TPU v7x, 32 devices: a whole 2x2x4 slice. The times are simulated.
32 devices in a mesh: rows: 4 (over z), cols: 2 (over y), dp: 4 (over x, core).
Axes of the slice: x: 2, y: 2, z: 4, core: 2. Of those that a mesh axis runs over, the one named last changes fastest.
Arguments:
- features: bfloat16 [4, 32, 512, 256], P('dp', 'rows', 'cols'), may hold values from -340 to 340, as said below
- upstream: bfloat16 [4, 32, 512, 256], P('dp', 'rows', 'cols'), may hold values from -6 to 6
- conv_weight: bfloat16 [3, 3, 32, 256], replicated, may hold values from -0.375 to 0.375
- norm_gain: float32 [256], replicated, may hold values from 0.25 to 1.75
- norm_bias: float32 [256], replicated, may hold values from -3 to 3
Outputs:
- input_grad: bfloat16 [4, 32, 512, 256], P('dp', 'rows', 'cols')
- weight_grad: float32 [3, 3, 32, 256], replicated
- gain_grad: float32 [256], replicated
- bias_grad: float32 [256], replicated
Inputs may be any that keep to these rules, and one draw needn't show every extreme that they name: `features`: finite feature values.
All inputs are finite; a program needn't handle non-finite values.
Results may differ from a plain program's by a relative error of at most 0.0031.
Values may be sent and summed in bfloat16 or wider, within the bound.
No kernel may reach another device: no remote copies, remote signals or barrier semaphores. Data moves between devices by JAX's collectives and lax.ppermute only.
A program may use at most 128 MiB of HBM per device.

v0:
```python
import math

import jax
import jax.numpy as jnp
from jax import lax
from jax.sharding import PartitionSpec as P

C = 256
CHANNEL_GROUPS = 8
GS = 32
DILATION_RATE = 6
ITERS = 5


EPSILON = 1e-05


def padded(shard, sides, width):
    for axis, dim in sides:
        size, length = (lax.axis_size(axis), shard.shape[dim])
        up = [(i, (i + 1) % size) for i in range(size - 1)]
        down = [(j, i) for i, j in up]
        last = lax.slice_in_dim(shard, length - width, length, axis=dim)
        leading = lax.slice_in_dim(shard, 0, width, axis=dim)
        before = lax.ppermute(last, axis, up)
        after = lax.ppermute(leading, axis, down)
        shard = jnp.concatenate([before, shard, after], axis=dim)
    return shard


def whitening_matrix(covariance):
    trace_sum = jnp.trace(covariance, axis1=1, axis2=2)
    normed = covariance / trace_sum[:, None, None]
    identity = jnp.broadcast_to(jnp.eye(GS, dtype=jnp.float32), covariance.shape)
    iterate = identity
    for repeat in range(ITERS):
        product = jnp.einsum("gij,gjk->gik", iterate, iterate, precision=lax.Precision.HIGHEST)
        product = jnp.einsum("gij,gjk->gik", product, iterate, precision=lax.Precision.HIGHEST)
        product = jnp.einsum("gij,gjk->gik", product, normed, precision=lax.Precision.HIGHEST)
        iterate = 1.5 * iterate - 0.5 * product
    return iterate / jnp.sqrt(trace_sum)[:, None, None]


def dilated_conv(border_filled, filter_weight):
    return lax.conv_general_dilated(
        border_filled,
        filter_weight,
        (1, 1),
        "VALID",
        rhs_dilation=(DILATION_RATE, DILATION_RATE),
        dimension_numbers=("NHWC", "HWIO", "NHWC"),
        feature_group_count=CHANNEL_GROUPS,
        preferred_element_type=jnp.float32,
    )


def flipped_kernel(filter_weight):
    reordered = filter_weight.reshape(3, 3, GS, CHANNEL_GROUPS, GS)[::-1, ::-1]
    return jnp.transpose(reordered, (0, 1, 4, 3, 2)).reshape(3, 3, GS, C)


def upstream_taps(activation, border_upstream):
    row_count = activation.shape[1]
    column_count = activation.shape[2]
    act_groups = activation.reshape(activation.shape[:3] + (CHANNEL_GROUPS, GS))
    tap_list = []
    for row_offset in range(3):
        for column_offset in range(3):
            row_begin = (2 - row_offset) * DILATION_RATE
            column_begin = (2 - column_offset) * DILATION_RATE
            sliding_patch = border_upstream[
                :, row_begin : row_begin + row_count, column_begin : column_begin + column_count, :
            ]
            sliding_patch = sliding_patch.reshape(act_groups.shape)
            tap_grad = jnp.einsum(
                "bhwgi,bhwgo->igo", act_groups, sliding_patch, preferred_element_type=jnp.float32
            )
            tap_list.append(tap_grad.reshape(GS, C))
    return jnp.stack(tap_list).reshape(3, 3, GS, C)


def shards(features, upstream, conv_weight, norm_gain, norm_bias):
    mos_n, row_count, column_count, channels = features.shape
    rows_all = row_count * lax.axis_size("rows")
    cols_all = column_count * lax.axis_size("cols")
    cell_count = mos_n * rows_all * cols_all * lax.axis_size("dp")
    grouped = features.reshape(mos_n, row_count, column_count, CHANNEL_GROUPS, GS)
    identity = jnp.eye(GS, dtype=jnp.float32)
    local_sum = jnp.sum(grouped.astype(jnp.float32), axis=(0, 1, 2))
    channel_mean = lax.psum(local_sum, ("rows", "cols", "dp")) / cell_count
    centered = grouped.astype(jnp.float32) - channel_mean
    local_cov = jnp.einsum("bhwgi,bhwgj->gij", centered, centered, precision=lax.Precision.HIGHEST)
    covariance = lax.psum(local_cov, ("rows", "cols", "dp")) / cell_count + EPSILON * identity
    whitener, pullback = jax.vjp(whitening_matrix, covariance)
    gain_group = norm_gain.reshape(CHANNEL_GROUPS, GS)
    bias_group = norm_bias.reshape(CHANNEL_GROUPS, GS)
    border_upstream = padded(upstream, (("rows", 1), ("cols", 2)), DILATION_RATE)
    white_part = jnp.einsum("goi,bhwgi->bhwgo", whitener, centered, precision=lax.Precision.HIGHEST)
    pre_part = gain_group * white_part + bias_group
    act_part = jax.nn.silu(pre_part).reshape(centered.shape[:3] + (C,)).astype(jnp.bfloat16)
    weight_local = upstream_taps(act_part, border_upstream)
    act_grad = dilated_conv(border_upstream, flipped_kernel(conv_weight)).reshape(
        mos_n, row_count, column_count, CHANNEL_GROUPS, GS
    )
    sigmoid_value = jax.nn.sigmoid(pre_part)
    pre_grad = act_grad * (sigmoid_value * (1.0 + pre_part * (1.0 - sigmoid_value)))
    gain_local = jnp.sum(pre_grad * white_part, axis=(0, 1, 2))
    bias_local = jnp.sum(pre_grad, axis=(0, 1, 2))
    white_grad = pre_grad * gain_group
    whitener_local = jnp.einsum(
        "bhwgo,bhwgi->goi", white_grad, centered, precision=lax.Precision.HIGHEST
    )
    tap_sum, gain_sum, bias_sum, whitener_grad = lax.psum(
        (weight_local, gain_local, bias_local, whitener_local), ("rows", "cols", "dp")
    )
    cov_grad = pullback(whitener_grad)[0]
    symmetric = cov_grad + jnp.swapaxes(cov_grad, 1, 2)
    back_term = jnp.einsum(
        "goi,bhwgo->bhwgi", whitener, white_grad, precision=lax.Precision.HIGHEST
    )
    mean_term = (
        jnp.einsum("goi,go->gi", whitener, gain_group * bias_sum, precision=lax.Precision.HIGHEST)
        / cell_count
    )
    cov_term = (
        jnp.einsum("gij,bhwgj->bhwgi", symmetric, centered, precision=lax.Precision.HIGHEST)
        / cell_count
    )
    input_grad = (
        (back_term - mean_term + cov_term)
        .reshape(mos_n, row_count, column_count, channels)
        .astype(jnp.bfloat16)
    )
    grad_scale = 1.0 / math.sqrt(cell_count)
    return (
        input_grad,
        tap_sum * grad_scale,
        gain_sum.reshape(C) * grad_scale,
        bias_sum.reshape(C) * grad_scale,
    )


def solution(mesh):
    placed = (P("dp", "rows", "cols", None), P("dp", "rows", "cols", None), P(), P(), P())
    return jax.shard_map(
        shards,
        mesh=mesh,
        in_specs=placed,
        out_specs=(P("dp", "rows", "cols", None), P(), P(), P()),
        check_vma=False,
    )
```

profile of v0, /device:TPU:0, one launch (start us, length us, event | category | flops | bytes accessed | tf_op | source)
XLA Modules:
  0.0 539.0 jit_solution(13832118938008311129)
XLA Ops:
  7.2 1.5 copy.161
  10.0 5.0 collective-permute-start
  16.9 1.5 copy.170
  18.7 41.8 %psum.42 = f32[8,32]{1,0:T(8,128)S(1)} all-reduce(f32[8,32]{1,0:T(8,128)S(1)} %reduce_sum.66), channel_id=1, replica_groups=mesh['rows'=4,'cols'=2,'dp'=4] {'rows','cols','dp'}, use_global_device_ids=true, to_apply=%region_1.0 | all-reduce | flops 256 | bytes 2048 | tf_op jit(solution)/shard_map/psum | solution.py:90
  60.5 2.4 convolution_bitcast_fusion.2
  62.8 41.8 %psum.43 = f32[8,32,32]{2,1,0:T(8,128)S(1)} all-reduce(f32[8,32,32]{2,1,0:T(8,128)S(1)} %convolution_bitcast_fusion.2), channel_id=1, replica_groups=mesh['rows'=4,'cols'=2,'dp'=4] {'rows','cols','dp'}, use_global_device_ids=true, to_apply=%region_2.0 | all-reduce | flops 8192 | bytes 65536 | tf_op jit(solution)/shard_map/psum | solution.py:93
  111.8 1.7 pad_maximum_fusion.1
  113.5 2.1 fusion.81
  115.7 1.9 copy.164
  117.6 4.8 collective-permute-start.2
  122.4 2.5 copy.165
  124.9 1.7 collective-permute-start.3
  126.6 3.4 fusion.42
  130.0 2.1 reshape.175
  132.8 2.5 copy.166
  135.3 2.5 copy.167
  137.8 6.1 %pad_maximum_fusion = bf16[1,20,268,256]{2,3,1,0:T(8,128)(2,1)} fusion(bf16[1,20,6,256]{2,3,1,0:T(8,128)(2,1)} %copy.167, bf16[1,6,256,256]{2,3,1,0:T(8,128)(2,1)} %collective-permute-done.1, bf16[1,8,256,256]{2,3,1,0:T(8,128)(2,1)S(1)} %copy.161, bf16[1,6,256,256]{2,3,1,0:T(8,128)(2,1)S(1)} %collective-permute-done, bf16[1,20,6,256]{2,3,1,0:T(8,128)(2,1)} %copy.166), kind=kLoop, calls=%fused_computation | loop fusion | flops 13721600 | bytes 5488640 | tf_op jit(solution)/shard_map/concatenate | solution.py:27
  143.9 47.7 %copy.168 = bf16[1,20,268,8,32]{4,0,3,2,1:T(2,128)(2,1)} copy(bf16[1,20,268,8,32]{2,4,3,1,0:T(8,128)(2,1)} %bitcast.220) | data formatting | bytes 5488640 | tf_op jit(solution)/shard_map/concatenate | solution.py:27
  191.6 79.8 %fusion.36 = f32[1,8,256,8,32]{4,0,3,2,1:T(1,128)} fusion(bf16[1,20,268,8,32]{4,0,3,2,1:T(2,128)(2,1)} %copy.168, bf16[3,3,32,8,32]{4,3,2,1,0:T(8,128)(2,1)S(1)} %copy-done.27), kind=kOutput, calls=%fused_computation.79 | convolution fusion | flops 301989888 | bytes 4988928 | tf_op jit(solution)/shard_map/conv_general_dilated | solution.py:45
  271.4 19.1 %copy.177 = f32[1,8,256,8,32]{2,4,3,1,0:T(8,128)} copy(f32[1,8,256,8,32]{4,0,3,2,1:T(1,128)} %fusion.36) | data formatting | bytes 4194304 | tf_op jit(solution)/shard_map/conv_general_dilated | solution.py:45
  290.6 4.1 fusion.1
  294.6 1.4 copy-done
  296.0 3.0 convolution_bitcast_fusion.1
  298.9 51.0 %all-reduce = (f32[8,32]{1,0:T(8,128)}, f32[8,32,32]{2,1,0:T(8,128)}, f32[8,32]{1,0:T(8,128)}) all-reduce(f32[8,32]{1,0:T(8,128)} %get-tuple-element.17, f32[8,32,32]{2,1,0:T(8,128)} %convolution_bitcast_fusion.1, f32[8,32]{1,0:T(8,128)S(1)} %get-tuple-element.16), channel_id=1, replica_groups=mesh['rows'=4,'cols'=2,'dp'=4] {'rows','cols','dp'}, use_global_device_ids=true, to_apply=%region_5.6 | all-reduce | flops 8704 | bytes 69632 | tf_op jit(solution)/shard_map/psum | solution.py:113
  349.9 1.4 fusion.47
  352.6 1.4 convolution_add_fusion.15
  354.0 1.3 convolution_add_fusion.14
  362.5 3.4 fusion.5
  365.9 5.0 pad_maximum_fusion.2
  372.1 1.6 fusion.21
  374.4 5.4 pad_maximum_fusion.6
  380.9 1.6 fusion.25
  383.2 1.6 fusion.28
  385.5 1.6 fusion.30
  387.8 1.6 fusion.32
  390.1 1.6 fusion.34
  392.4 1.4 constant_dynamic-update-slice_fusion.8
  394.5 1.5 constant_dynamic-update-slice_fusion.7
  396.0 1.4 constant_dynamic-update-slice_fusion.6
  397.4 1.4 constant_dynamic-update-slice_fusion.5
  399.4 1.4 constant_dynamic-update-slice_fusion.3
  400.7 1.4 constant_dynamic-update-slice_fusion.2
  402.1 1.4 constant_dynamic-update-slice_fusion.1
  403.5 1.4 constant_dynamic-update-slice_fusion
  410.1 3.9 fusion.9
  414.1 1.3 copy.213
  416.7 113.5 %all-reduce.3.cloned.1.call-done = f32[3,3,32,256]{3,2,1,0:T(8,128)} async-done(((f32[3,3,32,256]{3,2,1,0:T(8,128)}), f32[3,3,32,256]{3,2,1,0:T(8,128)}) %all-reduce.3.cloned.1.call-update) | async-done | bytes 294928 | tf_op jit(solution)/shard_map/psum | solution.py:113
  530.2 1.7 broadcast_multiply_fusion
  (188 shorter events, 33.2 us)
Async XLA Ops:
  7.2 523.1 %all-reduce.3.cloned.1.call-start = ((), (), s32[]{:S(2)}) async-start(), calls=%async_computation | async-start | bytes 589824 | tf_op jit(solution)/shard_map/psum | solution.py:113
  10.0 101.8 %collective-permute-start = (bf16[1,6,256,256]{2,3,1,0:T(8,128)(2,1)}, bf16[1,6,256,256]{2,3,1,0:T(8,128)(2,1)S(1)}, u32[]{:S(2)}, u32[]{:S(2)}) collective-permute-start(bf16[1,6,256,256]{2,3,1,0:T(8,128)(2,1)} %get-tuple-element.33), channel_id=1, source_target_pairs={{0,8},{8,16},{16,24},{1,9},{9,17},{17,25},{2,10},{10,18},{18,26},{... | collective-permute-start | bytes 2359304 | tf_op jit(solution)/shard_map/ppermute | solution.py:25
  15.0 96.8 %collective-permute-start.1 = (bf16[1,6,256,256]{2,3,1,0:T(8,128)(2,1)}, bf16[1,6,256,256]{2,3,1,0:T(8,128)(2,1)}, u32[]{:S(2)}, u32[]{:S(2)}) collective-permute-start(bf16[1,6,256,256]{2,3,1,0:T(8,128)(2,1)} %get-tuple-element.34), channel_id=1, source_target_pairs={{8,0},{16,8},{24,16},{9,1},{17,9},{25,17},{10,2},{18,10},{26,18},{... | collective-permute-start | bytes 2359304 | tf_op jit(solution)/shard_map/ppermute | solution.py:26
  105.7 5.0 copy-start.41
  106.3 2.7 copy-start.8
  107.5 4.3 copy-start.31
  109.0 2.7 copy-start.12
  109.3 2.5 copy-start.33
  109.7 3.9 copy-start.5
  110.2 16.3 %copy-start.44 = (f32[8]{0:T(128)}, f32[8]{0:T(128)S(1)}, u32[]{:S(2)}) copy-start(f32[8]{0:T(128)S(1)} %get-tuple-element.41) | copy-start | bytes 100
  110.5 3.1 copy-start.7
  111.8 26.0 %copy-start.2 = (bf16[1,6,256,256]{2,3,1,0:T(8,128)(2,1)}, bf16[1,6,256,256]{2,3,1,0:T(8,128)(2,1)S(1)}, u32[]{:S(2)}) copy-start(bf16[1,6,256,256]{2,3,1,0:T(8,128)(2,1)S(1)} %collective-permute-done) | copy-start | bytes 2359300
  115.7 10.9 %copy-start.24 = (f32[8,32,32]{2,1,0:T(8,128)S(1)}, f32[8,32,32]{2,1,0:T(8,128)}, u32[]{:S(2)}) copy-start(f32[8,32,32]{2,1,0:T(8,128)} %fusion.14) | copy-start | bytes 98308
  117.6 15.2 %collective-permute-start.2 = (bf16[1,20,6,256]{3,1,2,0:T(8,128)(2,1)S(1)}, bf16[1,20,6,256]{3,1,2,0:T(8,128)(2,1)}, u32[]{:S(2)}, u32[]{:S(2)}) collective-permute-start(bf16[1,20,6,256]{3,1,2,0:T(8,128)(2,1)S(1)} %copy.164), channel_id=1, source_target_pairs={{0,4},{1,5},{2,6},{3,7},{8,12},{9,13},{10,14},{11,15},{16,20},{17,... | collective-permute-start | bytes 184328 | tf_op jit(solution)/shard_map/ppermute | solution.py:25
  124.9 7.2 %copy-start.50 = (f32[256]{0:T(256)S(1)}, f32[256]{0:T(256)}, u32[]{:S(2)}) copy-start(f32[256]{0:T(256)} %param.8) | copy-start | bytes 3076
  124.9 7.3 %copy-start.51 = (f32[256]{0:T(256)S(1)}, f32[256]{0:T(256)}, u32[]{:S(2)}) copy-start(f32[256]{0:T(256)} %param.9) | copy-start | bytes 3076
  124.9 10.4 %collective-permute-start.3 = (bf16[1,20,6,256]{3,1,2,0:T(8,128)(2,1)}, bf16[1,20,6,256]{3,1,2,0:T(8,128)(2,1)}, u32[]{:S(2)}, u32[]{:S(2)}) collective-permute-start(bf16[1,20,6,256]{3,1,2,0:T(8,128)(2,1)} %copy.165), channel_id=1, source_target_pairs={{4,0},{5,1},{6,2},{7,3},{12,8},{13,9},{14,10},{15,11},{20,16},{21,... | collective-permute-start | bytes 184328 | tf_op jit(solution)/shard_map/ppermute | solution.py:26
  143.9 47.7 %copy-start.27 = (bf16[3,3,32,8,32]{4,3,2,1,0:T(8,128)(2,1)S(1)}, bf16[3,3,32,8,32]{4,3,2,1,0:T(8,128)(2,1)}, u32[]{:S(2)}) copy-start(bf16[3,3,32,8,32]{4,3,2,1,0:T(8,128)(2,1)} %reshape.175) | copy-start | bytes 442372
  349.9 5.4 %copy-start.6 = (f32[8,32,32]{2,1,0:T(8,128)S(1)}, f32[8,32,32]{2,1,0:T(8,128)}, u32[]{:S(2)}) copy-start(f32[8,32,32]{2,1,0:T(8,128)} %copy-done.5) | copy-start | bytes 98308
  349.9 5.8 %copy-start.16 = (f32[8,32,32]{2,1,0:T(8,128)S(1)}, f32[8,32,32]{2,1,0:T(8,128)}, u32[]{:S(2)}) copy-start(f32[8,32,32]{2,1,0:T(8,128)} %copy-done.14) | copy-start | bytes 98308
  349.9 5.8 %copy-start.42 = (f32[8]{0:T(128)S(1)}, f32[8]{0:T(128)}, u32[]{:S(2)}) copy-start(f32[8]{0:T(128)} %copy-done.41) | copy-start | bytes 100
  349.9 6.5 %copy-start.13 = (f32[8,32,32]{2,1,0:T(8,128)S(1)}, f32[8,32,32]{2,1,0:T(8,128)}, u32[]{:S(2)}) copy-start(f32[8,32,32]{2,1,0:T(8,128)} %copy-done.12) | copy-start | bytes 98308
  354.0 4.4 copy-start.11
  355.7 3.5 copy-start.18
  356.9 3.5 copy-start.9
  357.3 4.1 copy-start.28
  357.3 4.1 copy-start.38
  357.3 4.1 copy-start.45
  357.7 3.7 copy-start.20
  357.7 4.8 copy-start.1
  357.7 4.8 copy-start.25
  362.5 3.4 copy-start.3
  362.5 3.4 copy-start.4
  393.8 13.9 %copy-start.19 = (f32[8,32,32]{2,1,0:T(8,128)S(1)}, f32[8,32,32]{2,1,0:T(8,128)}, u32[]{:S(2)}) copy-start(f32[8,32,32]{2,1,0:T(8,128)} %copy-done.18) | copy-start | bytes 98308
  394.2 13.6 %copy-start.34 = (f32[8,32,32]{2,1,0:T(8,128)S(1)}, f32[8,32,32]{2,1,0:T(8,128)}, u32[]{:S(2)}) copy-start(f32[8,32,32]{2,1,0:T(8,128)} %copy-done.33) | copy-start | bytes 98308
  394.2 13.6 %copy-start.39 = (f32[8,32,32]{2,1,0:T(8,128)S(1)}, f32[8,32,32]{2,1,0:T(8,128)}, u32[]{:S(2)}) copy-start(f32[8,32,32]{2,1,0:T(8,128)} %fusion.48) | copy-start | bytes 98308
  394.2 14.0 %copy-start.21 = (f32[8,32,32]{2,1,0:T(8,128)S(1)}, f32[8,32,32]{2,1,0:T(8,128)}, u32[]{:S(2)}) copy-start(f32[8,32,32]{2,1,0:T(8,128)} %copy-done.20) | copy-start | bytes 98308
  394.2 14.0 %copy-start.32 = (f32[8,32,32]{2,1,0:T(8,128)S(1)}, f32[8,32,32]{2,1,0:T(8,128)}, u32[]{:S(2)}) copy-start(f32[8,32,32]{2,1,0:T(8,128)} %copy-done.31) | copy-start | bytes 98308
  394.3 14.4 %copy-start.23 = (f32[8,32,32]{2,1,0:T(8,128)S(1)}, f32[8,32,32]{2,1,0:T(8,128)}, u32[]{:S(2)}) copy-start(f32[8,32,32]{2,1,0:T(8,128)} %copy-done.22) | copy-start | bytes 98308
  394.3 14.4 %copy-start.30 = (f32[8,32,32]{2,1,0:T(8,128)S(1)}, f32[8,32,32]{2,1,0:T(8,128)}, u32[]{:S(2)}) copy-start(f32[8,32,32]{2,1,0:T(8,128)} %copy-done.29) | copy-start | bytes 98308
  394.3 14.7 %copy-start.17 = (f32[8,32,32]{2,1,0:T(8,128)S(1)}, f32[8,32,32]{2,1,0:T(8,128)}, u32[]{:S(2)}) copy-start(f32[8,32,32]{2,1,0:T(8,128)} %copy-done.14) | copy-start | bytes 98308
  394.3 14.7 %copy-start.36 = (f32[8,32,32]{2,1,0:T(8,128)S(1)}, f32[8,32,32]{2,1,0:T(8,128)}, u32[]{:S(2)}) copy-start(f32[8,32,32]{2,1,0:T(8,128)} %copy-done.35) | copy-start | bytes 98308
  394.3 14.7 %copy-start.43 = (f32[8]{0:T(128)S(1)}, f32[8]{0:T(128)}, u32[]{:S(2)}) copy-start(f32[8]{0:T(128)} %copy-done.41) | copy-start | bytes 100
  394.3 14.7 %copy-start.49 = (f32[8]{0:T(128)S(1)}, f32[8]{0:T(128)}, u32[]{:S(2)}) copy-start(f32[8]{0:T(128)} %get-tuple-element.40) | copy-start | bytes 100
  403.5 6.2 %copy-start.48 = (f32[8,32]{1,0:T(8,128)S(1)}, f32[8,32]{1,0:T(8,128)}, u32[]{:S(2)}) copy-start(f32[8,32]{1,0:T(8,128)} %get-tuple-element.18) | copy-start | bytes 3076
  403.5 6.2 %copy-start.26 = (f32[8,32,32]{2,1,0:T(8,128)S(1)}, f32[8,32,32]{2,1,0:T(8,128)}, u32[]{:S(2)}) copy-start(f32[8,32,32]{2,1,0:T(8,128)} %fusion.14) | copy-start | bytes 98308
  403.5 6.2 %copy-start.46 = (f32[8]{0:T(128)S(1)}, f32[8]{0:T(128)}, u32[]{:S(2)}) copy-start(f32[8]{0:T(128)} %copy-done.44) | copy-start | bytes 100
  404.9 5.1 copy-start.40
  (9 other events, 14.6 us)
Sparse Core Ops, SparseCore 0:
  405.0 125.1 all-reduce.2
where the time goes:
time: 549 us; the launch traced here: 539 us
  blocking collectives  135 us (25%)
  matrix products  128 us (23%)
  waiting for transfers between devices  114 us (21%)
  local copies, waits for them, and re-layouts  108 us (20%)
  other arithmetic  26.7 us (5%)
  between operations  15.3 us (3%)
  starting transfers between devices  12.8 us (2%)
    psum x1, waiting for transfers between devices, shards(): lax.psum((weight_local, gain_local, bias_local, whitener_local), ('rows',...  114 us
    conv_general_dilated x1, matrix products, dilated_conv(): lax.conv_general_dilated(border_filled, filter_weight, (1, 1), 'VALID', r...  79.8 us
    psum x1, blocking collectives, shards(): lax.psum((weight_local, gain_local, bias_local, whitener_local), ('rows',...  51 us
    concatenate x1, local copies, waits for them, and re-layouts, padded(): shard = jnp.concatenate([before, shard, after], axis=dim)  47.7 us
    psum x1, blocking collectives, shards(): lax.psum(local_cov, ('rows', 'cols', 'dp')) / cell_count  41.8 us
    psum x1, blocking collectives, shards(): channel_mean = lax.psum(local_sum, ('rows', 'cols', 'dp')) / cell_count  41.8 us
    conv_general_dilated x1, local copies, waits for them, and re-layouts, dilated_conv(): lax.conv_general_dilated(border_filled, filter_weight, (1, 1), 'VALID', r...  19.1 us
    concatenate x4, other arithmetic, padded(): shard = jnp.concatenate([before, shard, after], axis=dim)  18.2 us
  transfers between devices with their start and end apart: 5, of which 1 were waited for; matrix products, arithmetic and copies ran while one was open for 6% of the time, Pallas kernels for 0%

commit v1 on v0

v1 whole, which is shorter than its diff:
```python
import functools
import math

import jax
import jax.numpy as jnp
from jax import lax
from jax.experimental import pallas as pl
from jax.experimental.pallas import tpu as pltpu
from jax.sharding import PartitionSpec as P

C = 256
CHANNEL_GROUPS = 8
GS = 32
DILATION_RATE = 6
ITERS = 5
EPSILON = 1e-05

F32 = jnp.float32
BF16 = jnp.bfloat16
VMEM_SPEC = pl.BlockSpec(memory_space=pltpu.VMEM)


def run(body, out_shapes, operands, scratch=(), limit=40, flops=0):
    many = isinstance(out_shapes, (tuple, list))
    return pl.pallas_call(
        body,
        out_shape=out_shapes,
        in_specs=[VMEM_SPEC] * len(operands),
        out_specs=[VMEM_SPEC] * len(out_shapes) if many else VMEM_SPEC,
        scratch_shapes=list(scratch),
        compiler_params=pltpu.CompilerParams(vmem_limit_bytes=limit * 2**20),
        cost_estimate=pl.CostEstimate(flops=flops, bytes_accessed=2**20, transcendentals=0),
    )(*operands)


def same_group():
    rows = lax.broadcasted_iota(jnp.int32, (C, C), 0)
    columns = lax.broadcasted_iota(jnp.int32, (C, C), 1)
    return (rows >> 5) == (columns >> 5)


def fold(full, same):
    kept = jnp.where(same, full, 0.0)
    total = kept[0:GS]
    for g in range(1, CHANNEL_GROUPS):
        total = total + kept[g * GS : (g + 1) * GS]
    return total


def spread(packed, same):
    return jnp.where(same, jnp.concatenate([packed] * CHANNEL_GROUPS, axis=0), 0)


def split(value):
    high = value.astype(BF16)
    low = (value - high.astype(F32)).astype(BF16)
    return high, low


def spread_split(packed, same):
    high, low = split(spread(packed, same))
    return high, low


def dot(a, b):
    return jnp.dot(a, b, preferred_element_type=F32)


def times(left, right):
    rows = left.shape[0]
    left_high, left_low = split(left)
    right_high, right_low = right
    both = dot(jnp.concatenate([left_high, left_low], axis=0), right_high)
    return both[:rows] + both[rows:] + dot(left_high, right_low)


def unit():
    rows = lax.broadcasted_iota(jnp.int32, (GS, C), 0)
    columns = lax.broadcasted_iota(jnp.int32, (GS, C), 1)
    return jnp.where(rows == (columns & (GS - 1)), 1.0, 0.0)


def group_total(row, same):
    wide = jnp.broadcast_to(row, (8, C))
    return jnp.dot(wide, jnp.where(same, 1.0, 0.0), precision=lax.Precision.HIGHEST)


def stats_kernel(x_ref, out_ref):
    rows = x_ref.shape[0]
    cells = rows * x_ref.shape[1]
    same = same_group()

    def add_up(r, total):
        return total + jnp.sum(x_ref[r].astype(F32), axis=0, keepdims=True)

    mean = lax.fori_loop(0, rows, add_up, jnp.zeros((1, C), F32)) / cells

    def products(r, total):
        high, low = split(x_ref[r].astype(F32) - mean)
        return total + lax.dot_general(
            high,
            jnp.concatenate([high, low], axis=1),
            (((0,), (0,)), ((), ())),
            preferred_element_type=F32,
        )

    total = lax.fori_loop(0, rows, products, jnp.zeros((C, 2 * C), F32))
    cross = total[:, C:]
    out_ref[0:GS] = fold(total[:, :C] + cross + cross.T, same) / cells
    out_ref[GS : 2 * GS] = fold(jnp.broadcast_to(mean, (C, C)).T, same)
    out_ref[2 * GS : 2 * GS + 8] = jnp.broadcast_to(mean, (8, C))


def merge_kernel(a_ref, b_ref, out_ref):
    a, b = a_ref[...], b_ref[...]
    half = 0.5 * (a + b)
    gap = b - a
    wide = jnp.concatenate([gap[2 * GS :]] * (GS // 8), axis=0)
    out_ref[0:GS] = half[0:GS] + 0.25 * gap[GS : 2 * GS] * wide
    out_ref[GS:] = half[GS:]


def conv_kernel(up_ref, top_ref, bottom_ref, left_ref, right_ref, w_ref, moved_ref, out_ref, bands_ref, weight_ref):
    rows, width = up_ref.shape[0], up_ref.shape[1]
    d = DILATION_RATE
    pad = 16
    same = same_group()
    for tap in range(9):
        tile = jnp.concatenate([w_ref[tap].astype(F32)] * CHANNEL_GROUPS, axis=0)
        weight_ref[tap] = jnp.where(same, tile, 0.0).T.astype(BF16)
    moved_ref[1, 0:d] = top_ref[...]
    moved_ref[1, d : d + rows] = up_ref[...]
    moved_ref[1, d + rows :] = bottom_ref[...]
    line = lax.broadcasted_iota(jnp.int32, (width, C), 0)

    def shift(e, carry):
        band = moved_ref[1, e].astype(F32)
        bands_ref[pad : pad + width] = band
        bands_ref[pad - d : pad] = left_ref[e].astype(F32)
        bands_ref[pad + width : pad + width + d] = right_ref[e].astype(F32)
        moved_ref[0, e] = bands_ref[pad + d : pad + d + width].astype(BF16)
        moved_ref[2, e] = bands_ref[pad - d : pad - d + width].astype(BF16)
        return carry

    lax.fori_loop(0, rows + 2 * d, shift, 0)

    def row(r, carry):
        total = jnp.zeros((width, C), F32)
        for a in range(3):
            for b in range(3):
                total = total + dot(moved_ref[b, r + (2 - a) * d], weight_ref[3 * a + b])
        out_ref[r] = total
        return carry

    lax.fori_loop(0, rows, row, 0)


def main_kernel(x_ref, stats_ref, gain_ref, bias_ref, grad_ref, turned_ref, back_ref, sums_ref, kept_ref):
    rows = x_ref.shape[0]
    same = same_group()
    eye = unit()
    gain, bias = gain_ref[0:1], bias_ref[0:1]
    mean = stats_ref[2 * GS : 2 * GS + 1]
    cov = stats_ref[0:GS] + EPSILON * eye
    trace = group_total(jnp.sum(cov * eye, axis=0, keepdims=True), same)[0:1]
    normed = cov / trace
    normed_wide = spread_split(normed, same)
    iterate = 1.5 * eye - 0.5 * normed
    for k in range(ITERS - 1):
        wide = spread_split(iterate, same)
        square = times(iterate, wide)
        scaled = times(iterate, normed_wide)
        scaled_wide = spread_split(scaled, same)
        cube_scaled = times(square, scaled_wide)
        kept_ref[k, 0] = iterate
        kept_ref[k, 1] = square
        kept_ref[k, 2] = scaled
        kept_ref[k, 3] = times(iterate, scaled_wide)
        kept_ref[k, 4] = times(square, wide)
        iterate = 1.5 * iterate - 0.5 * cube_scaled
    whitener = iterate * lax.rsqrt(trace)
    kept_ref[ITERS - 1, 0] = whitener
    kept_ref[ITERS - 1, 1] = normed
    kept_ref[ITERS - 1, 2] = jnp.broadcast_to(trace, (GS, C))
    kept_ref[ITERS - 1, 3] = jnp.zeros((GS, C), F32)
    kept_ref[ITERS - 1, 4] = jnp.zeros((GS, C), F32)
    white_high, white_low = spread_split(whitener, same)
    mean_wide = jnp.broadcast_to(mean, (8, C))
    rounded = white_high.astype(F32) + white_low.astype(F32)
    offset = jnp.dot(mean_wide, rounded, precision=lax.Precision.HIGHEST)[0:1]
    kept_ref[ITERS - 1, 3, 0:8] = mean_wide

    def row(r, carry):
        gain_sum, bias_sum, products = carry
        x = x_ref[r]
        white = dot(x, white_high) + dot(x, white_low) - offset
        pre = gain * white + bias
        gate = 0.5 * jnp.tanh(0.5 * pre) + 0.5
        act = pre * gate
        turned_ref[r] = act.T.astype(BF16)
        pre_grad = grad_ref[r] * (gate + act * (1.0 - gate))
        gain_sum = gain_sum + jnp.sum(pre_grad * white, axis=0, keepdims=True)
        bias_sum = bias_sum + jnp.sum(pre_grad, axis=0, keepdims=True)
        high, low = split(pre_grad * gain)
        back_ref[r] = dot(high, white_high) + dot(low, white_high) + dot(high, white_low)
        products = products + lax.dot_general(
            x, jnp.concatenate([high, low], axis=1), (((0,), (0,)), ((), ())), preferred_element_type=F32
        )
        return gain_sum, bias_sum, products

    nothing = jnp.zeros((1, C), F32)
    gain_sum, bias_sum, products = lax.fori_loop(0, rows, row, (nothing, nothing, jnp.zeros((C, 2 * C), F32)))
    mean_column = jnp.broadcast_to(mean, (C, C)).T
    full = products[:, :C] + products[:, C:] - mean_column * (gain * bias_sum)
    sums_ref[0:GS] = fold(full + full.T, same)
    line = lax.broadcasted_iota(jnp.int32, (8, C), 0)
    sums_ref[GS : GS + 8] = jnp.where(line == 0, gain_sum, jnp.where(line == 1, bias_sum, 0.0))


def tap_kernel(turned_ref, moved_ref, out_ref, total_ref):
    rows = turned_ref.shape[0]
    d = DILATION_RATE
    total_ref[...] = jnp.zeros_like(total_ref)

    def row(r, carry):
        turned = turned_ref[r]
        for a in range(3):
            for b in range(3):
                total_ref[3 * a + b] += dot(turned, moved_ref[b, r + (2 - a) * d])
        return carry

    lax.fori_loop(0, rows, row, 0)
    same = same_group()
    for tap in range(9):
        out_ref[tap] = fold(total_ref[tap], same)


def final_kernel(cell_count, x_ref, back_ref, sums_ref, kept_ref, gain_ref, out_ref, vector_ref):
    rows = x_ref.shape[0]
    same = same_group()
    eye = unit()
    last = ITERS - 1
    whitener, normed = kept_ref[last, 0], kept_ref[last, 1]
    trace = kept_ref[last, 2, 0:1]
    mean = kept_ref[last, 3, 0:8]
    paired = sums_ref[0:GS]
    step = paired * lax.rsqrt(trace)
    step_wide = spread_split(step, same)
    normed_wide = spread_split(normed, same)
    change = -0.5 * step
    for k in range(ITERS - 1):
        iterate, square = kept_ref[k, 0], kept_ref[k, 1]
        scaled_wide = spread_split(kept_ref[k, 2], same)
        square_scaled_wide = spread_split(kept_ref[k, 3], same)
        moved = times(kept_ref[k, 4], step_wide) + times(change, square_scaled_wide)
        moved = moved + times(iterate, spread_split(times(change, scaled_wide), same))
        moved = moved + times(square, spread_split(times(change, normed_wide), same))
        change = 1.5 * change - 0.5 * moved
    inner = jnp.sum(change * normed + 0.5 * paired * whitener, axis=0, keepdims=True)
    symmetric = (change - eye * group_total(inner, same)[0:1]) / trace
    high, low = spread_split(symmetric * (1.0 / cell_count), same)
    rounded = high.astype(F32) + low.astype(F32)
    gain_sum, bias_sum = sums_ref[GS : GS + 1], sums_ref[GS + 1 : GS + 2]
    weighted = jnp.broadcast_to(gain_ref[0:1] * bias_sum * (1.0 / cell_count), (8, C))
    constant = jnp.dot(mean, rounded, precision=lax.Precision.HIGHEST)
    constant = constant + jnp.dot(weighted, spread(whitener, same), precision=lax.Precision.HIGHEST)
    constant = constant[0:1]

    def row(r, carry):
        x = x_ref[r]
        out_ref[r] = (dot(x, high) + dot(x, low) + back_ref[r] - constant).astype(BF16)
        return carry

    lax.fori_loop(0, rows, row, 0)
    vector_ref[...] = sums_ref[GS:] * (1.0 / math.sqrt(cell_count))


def stages(axes):
    for axis in axes:
        size = lax.axis_size(axis)
        stride = 1
        while stride < size:
            yield axis, [(i, i ^ stride) for i in range(size)]
            stride *= 2


def neighbours(axis):
    size = lax.axis_size(axis)
    up = [(i, i + 1) for i in range(size - 1)]
    return up, [(j, i) for i, j in up]


def shards(features, upstream, conv_weight, norm_gain, norm_bias):
    mos_n, rows, width, _ = features.shape
    axes = ("dp", "cols", "rows")
    cell_count = mos_n * rows * width
    for axis in axes:
        cell_count *= lax.axis_size(axis)
    d = DILATION_RATE
    x = features.reshape(rows, width, C)
    up = upstream.reshape(rows, width, C)
    gain = jnp.broadcast_to(norm_gain[None], (8, C))
    bias = jnp.broadcast_to(norm_bias[None], (8, C))

    forward, backward = neighbours("rows")
    top = lax.ppermute(up[rows - d :], "rows", forward)
    bottom = lax.ppermute(up[:d], "rows", backward)

    stats = run(stats_kernel, jax.ShapeDtypeStruct((2 * GS + 8, C), F32), (x,), flops=10**9)

    forward, backward = neighbours("cols")
    tall = lambda first, stop: jnp.concatenate([part[:, first:stop] for part in (top, up, bottom)], axis=0)
    left = lax.ppermute(tall(width - d, width), "cols", forward)
    right = lax.ppermute(tall(0, d), "cols", backward)

    for axis, pairs in stages(axes):
        other = lax.ppermute(stats, axis, pairs)
        stats = run(merge_kernel, jax.ShapeDtypeStruct(stats.shape, F32), (stats, other))

    moved, act_grad = run(
        conv_kernel,
        (
            jax.ShapeDtypeStruct((3, rows + 2 * d, width, C), BF16),
            jax.ShapeDtypeStruct((rows, width, C), F32),
        ),
        (up, top, bottom, left, right, conv_weight.reshape(9, GS, C)),
        scratch=(pltpu.VMEM((width + 32, C), F32), pltpu.VMEM((9, C, C), BF16)),
        flops=3 * 10**9,
    )
    turned, back, sums, kept = run(
        main_kernel,
        (
            jax.ShapeDtypeStruct((rows, C, width), BF16),
            jax.ShapeDtypeStruct((rows, width, C), F32),
            jax.ShapeDtypeStruct((GS + 8, C), F32),
            jax.ShapeDtypeStruct((ITERS, 5, GS, C), F32),
        ),
        (x, stats, gain, bias, act_grad),
        flops=3 * 10**9,
    )
    taps = run(
        tap_kernel,
        jax.ShapeDtypeStruct((9, GS, C), F32),
        (turned, moved),
        scratch=(pltpu.VMEM((9, C, C), F32),),
        flops=3 * 10**9,
    )
    for axis, pairs in stages(axes):
        sums = sums + lax.ppermute(sums, axis, pairs)
    for axis, pairs in stages(axes):
        taps = taps + lax.ppermute(taps, axis, pairs)
    input_grad, vectors = run(
        functools.partial(final_kernel, cell_count),
        (jax.ShapeDtypeStruct((rows, width, C), BF16), jax.ShapeDtypeStruct((8, C), F32)),
        (x, back, sums, kept, gain),
        flops=10**9,
    )
    return (
        input_grad.reshape(features.shape),
        (taps * (1.0 / math.sqrt(cell_count))).reshape(3, 3, GS, C),
        vectors[0],
        vectors[1],
    )


def solution(mesh):
    placed = (P("dp", "rows", "cols", None), P("dp", "rows", "cols", None), P(), P(), P())
    return jax.shard_map(
        shards,
        mesh=mesh,
        in_specs=placed,
        out_specs=(P("dp", "rows", "cols", None), P(), P(), P()),
        check_vma=False,
    )
```

time: 549 us -> 111 us (0.20); the launches traced: 539 us -> 111 us
  blocking collectives: 135 us -> 0 us
  matrix products: 128 us -> 0 us
  local copies, waits for them, and re-layouts: 108 us -> 2.19 us
  waiting for transfers between devices: 114 us -> 54 us
  Pallas kernels: 0 us -> 26.3 us
  other arithmetic: 26.7 us -> 1 us
  between operations: 15.3 us -> 0.89 us
  starting transfers between devices: 12.8 us -> 26.7 us
    psum x3 -> x0, blocking collectives: 135 us -> none  [the longest x1 51 us: shards(): lax.psum((weight_local, gain_local, bias_local, whitener_local), ('rows',...]
    psum x1 -> x0, waiting for transfers between devices: 114 us -> none  [shards(): lax.psum((weight_local, gain_local, bias_local, whitener_local), ('rows',...]
    conv_general_dilated x1 -> x0, matrix products: 79.8 us -> none  [dilated_conv(): lax.conv_general_dilated(border_filled, filter_weight, (1, 1), 'VALID', r...]
    ppermute x4 -> x19, waiting for transfers between devices: 0.01 us -> 54 us  [the longest x5 20 us: shards(): taps = taps + lax.ppermute(taps, axis, pairs)]
    dot_general x55 -> x0, matrix products: 48.6 us -> none  [the longest x9 10.9 us: upstream_taps(): jnp.einsum('bhwgi,bhwgo->igo', act_groups, sliding_patch, preferred_eleme...]
    concatenate x1 -> x0, local copies, waits for them, and re-layouts: 47.7 us -> none  [padded(): shard = jnp.concatenate([before, shard, after], axis=dim)]
    pallas_call x0 -> x10, Pallas kernels: none -> 26.3 us  [run(): pl.pallas_call(body, out_shape=out_shapes, in_specs=[VMEM_SPEC] * len(ope...]
    conv_general_dilated x1 -> x0, local copies, waits for them, and re-layouts: 19.1 us -> none  [dilated_conv(): lax.conv_general_dilated(border_filled, filter_weight, (1, 1), 'VALID', r...]
  transfers between devices with their start and end apart: 5 -> 19, of which waited for: 1 -> 15; matrix products, arithmetic and copies ran while one was open for 6% -> 1% of each run, Pallas kernels for 0% -> 8%
where the time goes in v1:
time: 111 us
  waiting for transfers between devices  54 us (49%)
  starting transfers between devices  26.7 us (24%)
  Pallas kernels  26.3 us (24%)
  local copies, waits for them, and re-layouts  2.19 us (2%)
    pallas_call x10, Pallas kernels, run(): pl.pallas_call(body, out_shape=out_shapes, in_specs=[VMEM_SPEC] * len(ope...  26.3 us
    ppermute x5, waiting for transfers between devices, shards(): taps = taps + lax.ppermute(taps, axis, pairs)  20 us
    ppermute x5, waiting for transfers between devices, shards(): sums = sums + lax.ppermute(sums, axis, pairs)  19.7 us
    ppermute x5, waiting for transfers between devices, shards(): other = lax.ppermute(stats, axis, pairs)  9.41 us
    ppermute x5, starting transfers between devices, shards(): other = lax.ppermute(stats, axis, pairs)  8.65 us
    ppermute x1, starting transfers between devices, shards(): top = lax.ppermute(up[rows - d:], 'rows', forward)  5.61 us
    ppermute x1, waiting for transfers between devices, shards(): right = lax.ppermute(tall(0, d), 'cols', backward)  4.33 us
    ppermute x5, starting transfers between devices, shards(): taps = taps + lax.ppermute(taps, axis, pairs)  4.3 us
  transfers between devices with their start and end apart: 19, of which 15 were waited for; matrix products, arithmetic and copies ran while one was open for 1% of the time, Pallas kernels for 8%

profile of v1, /device:TPU:0, one launch (start us, length us, event | category | flops | bytes accessed | tf_op | source)
XLA Modules:
  0.0 111.1 jit_solution(9171179890452232743)
XLA Ops:
  0.6 1.6 %slice_bitcast_fusion = (bf16[6,256,256]{2,1,0:T(8,128)(2,1)S(1)}, bf16[6,256,256]{2,1,0:T(8,128)(2,1)S(1)}) fusion(bf16[1,8,256,256]{3,2,1,0:T(8,128)(2,1)} %param.6), kind=kLoop, calls=%fused_computation | loop fusion | bytes 3145728 | tf_op jit(solution)/shard_map/slice | solution.py:307
  2.2 1.3 %collective-permute-start.6 = (bf16[6,256,256]{2,1,0:T(8,128)(2,1)S(1)}, bf16[6,256,256]{2,1,0:T(8,128)(2,1)S(1)}, u32[]{:S(2)}, u32[]{:S(2)}) collective-permute-start(bf16[6,256,256]{2,1,0:T(8,128)(2,1)S(1)} %get-tuple-element.22), channel_id=1, source_target_pairs={{8,0},{16,8},{24,16},{9,1},{17,9},{25,17},{10,2},{18,10},{26,18},{... | collective-permute-start | bytes 2359304 | tf_op jit(solution)/shard_map/ppermute | solution.py:307
  3.5 5.6 %collective-permute-start.5 = (bf16[6,256,256]{2,1,0:T(8,128)(2,1)S(1)}, bf16[6,256,256]{2,1,0:T(8,128)(2,1)S(1)}, u32[]{:S(2)}, u32[]{:S(2)}) collective-permute-start(bf16[6,256,256]{2,1,0:T(8,128)(2,1)S(1)} %get-tuple-element.23), channel_id=1, source_target_pairs={{0,8},{8,16},{16,24},{1,9},{9,17},{17,25},{2,10},{10,18},{18,26},{... | collective-permute-start | bytes 2359304 | tf_op jit(solution)/shard_map/ppermute | solution.py:306
  9.1 0.0 copy-start
  9.1 0.0 copy-start.2
  9.2 3.0 %shard_map.84.a_ref = f32[72,256]{1,0:T(8,128)S(1)} custom-call(bf16[8,256,256]{2,1,0:T(8,128)(2,1)S(1)} %bitcast.13), custom_call_target="tpu_custom_call" | custom-call | flops 1000000000 | bytes 1048576 | tf_op jit(solution)/shard_map/pallas_call | solution.py:25
  12.1 0.1 collective-permute-start
  12.2 1.3 %collective-permute-done.b_ref = f32[72,256]{1,0:T(8,128)S(1)} collective-permute-done((f32[72,256]{1,0:T(8,128)S(1)}, f32[72,256]{1,0:T(8,128)S(1)}, u32[]{:S(2)}, u32[]{:S(2)}) %collective-permute-start) | collective-permute-done | bytes 73760 | tf_op jit(solution)/shard_map/ppermute | solution.py:317
  13.5 2.0 %collective-permute-start.1 = (f32[72,256]{1,0:T(8,128)S(1)}, f32[72,256]{1,0:T(8,128)S(1)}, u32[]{:S(2)}, u32[]{:S(2)}) collective-permute-start(f32[72,256]{1,0:T(8,128)S(1)} %shard_map.85.a_ref), channel_id=1, source_target_pairs={{0,2},{1,3},{2,0},{3,1},{4,6},{5,7},{6,4},{7,5},{8,10},{9,11},{10,... | collective-permute-start | bytes 221192 | tf_op jit(solution)/shard_map/ppermute | solution.py:317
  15.5 2.6 %collective-permute-done.1.b_ref = f32[72,256]{1,0:T(8,128)S(1)} collective-permute-done((f32[72,256]{1,0:T(8,128)S(1)}, f32[72,256]{1,0:T(8,128)S(1)}, u32[]{:S(2)}, u32[]{:S(2)}) %collective-permute-start.1) | collective-permute-done | bytes 73760 | tf_op jit(solution)/shard_map/ppermute | solution.py:317
  18.1 1.9 %collective-permute-start.2 = (f32[72,256]{1,0:T(8,128)S(1)}, f32[72,256]{1,0:T(8,128)S(1)}, u32[]{:S(2)}, u32[]{:S(2)}) collective-permute-start(f32[72,256]{1,0:T(8,128)S(1)} %shard_map.86.a_ref), channel_id=1, source_target_pairs={{0,4},{4,0},{1,5},{5,1},{2,6},{6,2},{3,7},{7,3},{8,12},{12,8},{9,1... | collective-permute-start | bytes 221192 | tf_op jit(solution)/shard_map/ppermute | solution.py:317
  20.0 2.6 %collective-permute-done.2.b_ref = f32[72,256]{1,0:T(8,128)S(1)} collective-permute-done((f32[72,256]{1,0:T(8,128)S(1)}, f32[72,256]{1,0:T(8,128)S(1)}, u32[]{:S(2)}, u32[]{:S(2)}) %collective-permute-start.2) | collective-permute-done | bytes 73760 | tf_op jit(solution)/shard_map/ppermute | solution.py:317
  22.5 1.9 %collective-permute-start.3 = (f32[72,256]{1,0:T(8,128)S(1)}, f32[72,256]{1,0:T(8,128)S(1)}, u32[]{:S(2)}, u32[]{:S(2)}) collective-permute-start(f32[72,256]{1,0:T(8,128)S(1)} %shard_map.87.a_ref), channel_id=1, source_target_pairs={{0,8},{8,0},{16,24},{24,16},{1,9},{9,1},{17,25},{25,17},{2,10},{10... | collective-permute-start | bytes 221192 | tf_op jit(solution)/shard_map/ppermute | solution.py:317
  24.4 3.0 %collective-permute-done.3.b_ref = f32[72,256]{1,0:T(8,128)S(1)} collective-permute-done((f32[72,256]{1,0:T(8,128)S(1)}, f32[72,256]{1,0:T(8,128)S(1)}, u32[]{:S(2)}, u32[]{:S(2)}) %collective-permute-start.3) | collective-permute-done | bytes 73760 | tf_op jit(solution)/shard_map/ppermute | solution.py:317
  27.4 2.9 %collective-permute-start.4 = (f32[72,256]{1,0:T(8,128)S(1)}, f32[72,256]{1,0:T(8,128)S(1)}, u32[]{:S(2)}, u32[]{:S(2)}) collective-permute-start(f32[72,256]{1,0:T(8,128)S(1)} %shard_map.88.a_ref), channel_id=1, source_target_pairs={{0,16},{8,24},{16,0},{24,8},{1,17},{9,25},{17,1},{25,9},{2,18},{10... | collective-permute-start | bytes 221192 | tf_op jit(solution)/shard_map/ppermute | solution.py:317
  30.3 0.0 collective-permute-done.6.bottom_ref
  30.3 0.0 collective-permute-done.5.top_ref
  30.4 3.4 %collective-permute-start.7 = (bf16[20,6,256]{2,1,0:T(8,128)(2,1)S(1)}, bf16[20,6,256]{2,1,0:T(8,128)(2,1)S(1)}, u32[]{:S(2)}, u32[]{:S(2)}) collective-permute-start(bf16[20,6,256]{2,1,0:T(8,128)(2,1)S(1)} %pad_maximum_fusion), channel_id=1, source_target_pairs={{0,4},{1,5},{2,6},{3,7},{8,12},{9,13},{10,14},{11,15},{16,20},{17,... | collective-permute-start | bytes 184328 | tf_op jit(solution)/shard_map/ppermute | solution.py:313
  33.8 1.3 %collective-permute-start.8 = (bf16[20,6,256]{2,1,0:T(8,128)(2,1)S(1)}, bf16[20,6,256]{2,1,0:T(8,128)(2,1)S(1)}, u32[]{:S(2)}, u32[]{:S(2)}) collective-permute-start(bf16[20,6,256]{2,1,0:T(8,128)(2,1)S(1)} %pad_maximum_fusion.1), channel_id=1, source_target_pairs={{4,0},{5,1},{6,2},{7,3},{12,8},{13,9},{14,10},{15,11},{20,16},{21,... | collective-permute-start | bytes 184328 | tf_op jit(solution)/shard_map/ppermute | solution.py:314
  35.1 0.0 collective-permute-done.4.b_ref
  35.2 0.7 collective-permute-done.7.left_ref
  35.9 4.3 %collective-permute-done.8.right_ref = bf16[20,6,256]{2,1,0:T(8,128)(2,1)S(1)} collective-permute-done((bf16[20,6,256]{2,1,0:T(8,128)(2,1)S(1)}, bf16[20,6,256]{2,1,0:T(8,128)(2,1)S(1)}, u32[]{:S(2)}, u32[]{:S(2)}) %collective-permute-start.8) | collective-permute-done | bytes 61472 | tf_op jit(solution)/shard_map/ppermute | solution.py:314
  40.2 5.2 %shard_map.90 = (bf16[3,20,256,256]{3,2,1,0:T(8,128)(2,1)S(1)}, f32[8,256,256]{2,1,0:T(8,128)S(1)}) custom-call(bf16[8,256,256]{2,1,0:T(8,128)(2,1)S(1)} %bitcast.12, bf16[6,256,256]{2,1,0:T(8,128)(2,1)S(1)} %collective-permute-done.5.top_ref, bf16[6,256,256]{2,1,0:T(8,128)(2,1)S(1)} %collective-permute-done.6.bottom_ref, ...), custom_call_target="tpu_custom_call" | custom-call | flops 3000000000 | bytes 1048576 | tf_op jit(solution)/shard_map/pallas_call | solution.py:25
  45.4 8.1 %shard_map.91 = (bf16[8,256,256]{2,1,0:T(8,128)(2,1)S(1)}, f32[8,256,256]{2,1,0:T(8,128)S(1)}, f32[40,256]{1,0:T(8,128)S(1)}, f32[5,5,32,256]{3,2,1,0:T(8,128)S(1)}) custom-call(bf16[8,256,256]{2,1,0:T(8,128)(2,1)S(1)} %bitcast.14, f32[72,256]{1,0:T(8,128)S(1)} %shard_map.89.stats_ref, f32[8,256]{1,0:T(8,128)S(1)} %broadcast_in_dim.4.gain_ref, ...), custom_call_target="tpu_custom_call" | custom-call | flops 3000000000 | bytes 1048576 | tf_op jit(solution)/shard_map/pallas_call | solution.py:25
  53.5 4.2 %shard_map.93 = f32[9,32,256]{2,1,0:T(8,128)S(1)} custom-call(bf16[8,256,256]{2,1,0:T(8,128)(2,1)S(1)} %get-tuple-element.17.turned_ref, bf16[3,20,256,256]{3,2,1,0:T(8,128)(2,1)S(1)} %get-tuple-element.18.moved_ref), custom_call_target="tpu_custom_call" | custom-call | flops 3000000000 | bytes 1048576 | tf_op jit(solution)/shard_map/pallas_call | solution.py:25
  57.8 0.1 collective-permute-start.14
  57.8 1.6 %collective-permute-done.14 = f32[9,32,256]{2,1,0:T(8,128)S(1)} collective-permute-done((f32[9,32,256]{2,1,0:T(8,128)S(1)}, f32[9,32,256]{2,1,0:T(8,128)S(1)}, u32[]{:S(2)}, u32[]{:S(2)}) %collective-permute-start.14) | collective-permute-done | bytes 294944 | tf_op jit(solution)/shard_map/ppermute | solution.py:351
  59.5 1.5 %collective-permute-start.15 = (f32[9,32,256]{2,1,0:T(8,128)S(1)}, f32[9,32,256]{2,1,0:T(8,128)S(1)}, u32[]{:S(2)}, u32[]{:S(2)}) collective-permute-start(f32[9,32,256]{2,1,0:T(8,128)S(1)} %add.35), channel_id=1, source_target_pairs={{0,2},{1,3},{2,0},{3,1},{4,6},{5,7},{6,4},{7,5},{8,10},{9,11},{10,... | collective-permute-start | bytes 884744 | tf_op jit(solution)/shard_map/ppermute | solution.py:351
  61.0 7.6 %collective-permute-done.15 = f32[9,32,256]{2,1,0:T(8,128)S(1)} collective-permute-done((f32[9,32,256]{2,1,0:T(8,128)S(1)}, f32[9,32,256]{2,1,0:T(8,128)S(1)}, u32[]{:S(2)}, u32[]{:S(2)}) %collective-permute-start.15) | collective-permute-done | bytes 294944 | tf_op jit(solution)/shard_map/ppermute | solution.py:351
  68.6 0.1 collective-permute-start.16
  68.7 8.2 %collective-permute-done.16 = f32[9,32,256]{2,1,0:T(8,128)S(1)} collective-permute-done((f32[9,32,256]{2,1,0:T(8,128)S(1)}, f32[9,32,256]{2,1,0:T(8,128)S(1)}, u32[]{:S(2)}, u32[]{:S(2)}) %collective-permute-start.16) | collective-permute-done | bytes 294944 | tf_op jit(solution)/shard_map/ppermute | solution.py:351
  76.9 2.5 %collective-permute-start.17 = (f32[9,32,256]{2,1,0:T(8,128)S(1)}, f32[9,32,256]{2,1,0:T(8,128)S(1)}, u32[]{:S(2)}, u32[]{:S(2)}) collective-permute-start(f32[9,32,256]{2,1,0:T(8,128)S(1)} %add.37), channel_id=1, source_target_pairs={{0,8},{8,0},{16,24},{24,16},{1,9},{9,1},{17,25},{25,17},{2,10},{10... | collective-permute-start | bytes 884744 | tf_op jit(solution)/shard_map/ppermute | solution.py:351
  79.5 0.0 collective-permute-start.9
  79.5 1.2 %collective-permute-done.9 = f32[40,256]{1,0:T(8,128)S(1)} collective-permute-done((f32[40,256]{1,0:T(8,128)S(1)}, f32[40,256]{1,0:T(8,128)S(1)}, u32[]{:S(2)}, u32[]{:S(2)}) %collective-permute-start.9) | collective-permute-done | bytes 40992 | tf_op jit(solution)/shard_map/ppermute | solution.py:349
  80.7 1.5 %collective-permute-start.10 = (f32[40,256]{1,0:T(8,128)S(1)}, f32[40,256]{1,0:T(8,128)S(1)}, u32[]{:S(2)}, u32[]{:S(2)}) collective-permute-start(f32[40,256]{1,0:T(8,128)S(1)} %add.30), channel_id=1, source_target_pairs={{0,2},{1,3},{2,0},{3,1},{4,6},{5,7},{6,4},{7,5},{8,10},{9,11},{10,... | collective-permute-start | bytes 122888 | tf_op jit(solution)/shard_map/ppermute | solution.py:349
  82.2 2.5 %collective-permute-done.10 = f32[40,256]{1,0:T(8,128)S(1)} collective-permute-done((f32[40,256]{1,0:T(8,128)S(1)}, f32[40,256]{1,0:T(8,128)S(1)}, u32[]{:S(2)}, u32[]{:S(2)}) %collective-permute-start.10) | collective-permute-done | bytes 40992 | tf_op jit(solution)/shard_map/ppermute | solution.py:349
  84.7 0.3 collective-permute-start.11
  85.0 3.7 %collective-permute-done.11 = f32[40,256]{1,0:T(8,128)S(1)} collective-permute-done((f32[40,256]{1,0:T(8,128)S(1)}, f32[40,256]{1,0:T(8,128)S(1)}, u32[]{:S(2)}, u32[]{:S(2)}) %collective-permute-start.11) | collective-permute-done | bytes 40992 | tf_op jit(solution)/shard_map/ppermute | solution.py:349
  88.7 0.1 collective-permute-start.12
  88.8 3.9 %collective-permute-done.12 = f32[40,256]{1,0:T(8,128)S(1)} collective-permute-done((f32[40,256]{1,0:T(8,128)S(1)}, f32[40,256]{1,0:T(8,128)S(1)}, u32[]{:S(2)}, u32[]{:S(2)}) %collective-permute-start.12) | collective-permute-done | bytes 40992 | tf_op jit(solution)/shard_map/ppermute | solution.py:349
  92.8 0.3 collective-permute-start.13
  93.0 8.3 %collective-permute-done.13 = f32[40,256]{1,0:T(8,128)S(1)} collective-permute-done((f32[40,256]{1,0:T(8,128)S(1)}, f32[40,256]{1,0:T(8,128)S(1)}, u32[]{:S(2)}, u32[]{:S(2)}) %collective-permute-start.13) | collective-permute-done | bytes 40992 | tf_op jit(solution)/shard_map/ppermute | solution.py:349
  101.3 0.0 collective-permute-done.17
  101.4 0.1 collective-permute-start.18
  101.5 5.7 %shard_map.92 = (bf16[8,256,256]{2,1,0:T(8,128)(2,1)}, f32[8,256]{1,0:T(8,128)S(1)}) custom-call(bf16[8,256,256]{2,1,0:T(8,128)(2,1)S(1)} %bitcast.15, f32[8,256,256]{2,1,0:T(8,128)S(1)} %get-tuple-element.13.back_ref, f32[40,256]{1,0:T(8,128)S(1)} %add.34.sums_ref, f32[5,5,32,256]{3,2,1,0:T(8,128)S(1)} %get-tuple-element.15.kept_ref, ...), custom_call_target="tpu_custom_call" | custom-call | flops 1000000000 | bytes 1048576 | tf_op jit(solution)/shard_map/pallas_call | solution.py:25
  107.2 0.6 fusion.3
  107.8 2.6 %collective-permute-done.18 = f32[9,32,256]{2,1,0:T(8,128)S(1)} collective-permute-done((f32[9,32,256]{2,1,0:T(8,128)S(1)}, f32[9,32,256]{2,1,0:T(8,128)S(1)}, u32[]{:S(2)}, u32[]{:S(2)}) %collective-permute-start.18) | collective-permute-done | bytes 294944 | tf_op jit(solution)/shard_map/ppermute | solution.py:351
  110.4 0.8 add_multiply_fusion
  (29 shorter events, 0.4 us)
Async XLA Ops:
  0.6 8.5 %copy-start.1 = (bf16[1,8,256,256]{3,2,1,0:T(8,128)(2,1)S(1)}, bf16[1,8,256,256]{3,2,1,0:T(8,128)(2,1)}, u32[]{:S(2)}) copy-start(bf16[1,8,256,256]{3,2,1,0:T(8,128)(2,1)} %param.5) | copy-start | bytes 3145732
  2.2 28.1 %collective-permute-start.6 = (bf16[6,256,256]{2,1,0:T(8,128)(2,1)S(1)}, bf16[6,256,256]{2,1,0:T(8,128)(2,1)S(1)}, u32[]{:S(2)}, u32[]{:S(2)}) collective-permute-start(bf16[6,256,256]{2,1,0:T(8,128)(2,1)S(1)} %get-tuple-element.22), channel_id=1, source_target_pairs={{8,0},{16,8},{24,16},{9,1},{17,9},{25,17},{10,2},{18,10},{26,18},{... | collective-permute-start | bytes 2359304 | tf_op jit(solution)/shard_map/ppermute | solution.py:307
  3.5 26.8 %collective-permute-start.5 = (bf16[6,256,256]{2,1,0:T(8,128)(2,1)S(1)}, bf16[6,256,256]{2,1,0:T(8,128)(2,1)S(1)}, u32[]{:S(2)}, u32[]{:S(2)}) collective-permute-start(bf16[6,256,256]{2,1,0:T(8,128)(2,1)S(1)} %get-tuple-element.23), channel_id=1, source_target_pairs={{0,8},{8,16},{16,24},{1,9},{9,17},{17,25},{2,10},{10,18},{18,26},{... | collective-permute-start | bytes 2359304 | tf_op jit(solution)/shard_map/ppermute | solution.py:306
  9.1 15.3 %copy-start = (bf16[1,8,256,256]{3,2,1,0:T(8,128)(2,1)S(1)}, bf16[1,8,256,256]{3,2,1,0:T(8,128)(2,1)}, u32[]{:S(2)}) copy-start(bf16[1,8,256,256]{3,2,1,0:T(8,128)(2,1)} %param.6) | copy-start | bytes 3145732
  9.1 31.0 %copy-start.2 = (bf16[3,3,32,256]{3,2,1,0:T(8,128)(2,1)S(1)}, bf16[3,3,32,256]{3,2,1,0:T(8,128)(2,1)}, u32[]{:S(2)}) copy-start(bf16[3,3,32,256]{3,2,1,0:T(8,128)(2,1)} %param.7) | copy-start | bytes 442372
  12.1 1.3 %collective-permute-start = (f32[72,256]{1,0:T(8,128)S(1)}, f32[72,256]{1,0:T(8,128)S(1)}, u32[]{:S(2)}, u32[]{:S(2)}) collective-permute-start(f32[72,256]{1,0:T(8,128)S(1)} %shard_map.84.a_ref), channel_id=1, source_target_pairs={{0,1},{1,0},{2,3},{3,2},{4,5},{5,4},{6,7},{7,6},{8,9},{9,8},{10,11... | collective-permute-start | bytes 221192 | tf_op jit(solution)/shard_map/ppermute | solution.py:317
  13.5 4.6 %collective-permute-start.1 = (f32[72,256]{1,0:T(8,128)S(1)}, f32[72,256]{1,0:T(8,128)S(1)}, u32[]{:S(2)}, u32[]{:S(2)}) collective-permute-start(f32[72,256]{1,0:T(8,128)S(1)} %shard_map.85.a_ref), channel_id=1, source_target_pairs={{0,2},{1,3},{2,0},{3,1},{4,6},{5,7},{6,4},{7,5},{8,10},{9,11},{10,... | collective-permute-start | bytes 221192 | tf_op jit(solution)/shard_map/ppermute | solution.py:317
  18.1 4.4 %collective-permute-start.2 = (f32[72,256]{1,0:T(8,128)S(1)}, f32[72,256]{1,0:T(8,128)S(1)}, u32[]{:S(2)}, u32[]{:S(2)}) collective-permute-start(f32[72,256]{1,0:T(8,128)S(1)} %shard_map.86.a_ref), channel_id=1, source_target_pairs={{0,4},{4,0},{1,5},{5,1},{2,6},{6,2},{3,7},{7,3},{8,12},{12,8},{9,1... | collective-permute-start | bytes 221192 | tf_op jit(solution)/shard_map/ppermute | solution.py:317
  22.5 4.9 %collective-permute-start.3 = (f32[72,256]{1,0:T(8,128)S(1)}, f32[72,256]{1,0:T(8,128)S(1)}, u32[]{:S(2)}, u32[]{:S(2)}) collective-permute-start(f32[72,256]{1,0:T(8,128)S(1)} %shard_map.87.a_ref), channel_id=1, source_target_pairs={{0,8},{8,0},{16,24},{24,16},{1,9},{9,1},{17,25},{25,17},{2,10},{10... | collective-permute-start | bytes 221192 | tf_op jit(solution)/shard_map/ppermute | solution.py:317
  27.4 7.7 %collective-permute-start.4 = (f32[72,256]{1,0:T(8,128)S(1)}, f32[72,256]{1,0:T(8,128)S(1)}, u32[]{:S(2)}, u32[]{:S(2)}) collective-permute-start(f32[72,256]{1,0:T(8,128)S(1)} %shard_map.88.a_ref), channel_id=1, source_target_pairs={{0,16},{8,24},{16,0},{24,8},{1,17},{9,25},{17,1},{25,9},{2,18},{10... | collective-permute-start | bytes 221192 | tf_op jit(solution)/shard_map/ppermute | solution.py:317
  30.4 5.5 %collective-permute-start.7 = (bf16[20,6,256]{2,1,0:T(8,128)(2,1)S(1)}, bf16[20,6,256]{2,1,0:T(8,128)(2,1)S(1)}, u32[]{:S(2)}, u32[]{:S(2)}) collective-permute-start(bf16[20,6,256]{2,1,0:T(8,128)(2,1)S(1)} %pad_maximum_fusion), channel_id=1, source_target_pairs={{0,4},{1,5},{2,6},{3,7},{8,12},{9,13},{10,14},{11,15},{16,20},{17,... | collective-permute-start | bytes 184328 | tf_op jit(solution)/shard_map/ppermute | solution.py:313
  33.8 6.3 %collective-permute-start.8 = (bf16[20,6,256]{2,1,0:T(8,128)(2,1)S(1)}, bf16[20,6,256]{2,1,0:T(8,128)(2,1)S(1)}, u32[]{:S(2)}, u32[]{:S(2)}) collective-permute-start(bf16[20,6,256]{2,1,0:T(8,128)(2,1)S(1)} %pad_maximum_fusion.1), channel_id=1, source_target_pairs={{4,0},{5,1},{6,2},{7,3},{12,8},{13,9},{14,10},{15,11},{20,16},{21,... | collective-permute-start | bytes 184328 | tf_op jit(solution)/shard_map/ppermute | solution.py:314
  40.2 5.2 %copy-start.3 = (f32[256]{0:T(256)S(1)}, f32[256]{0:T(256)}, u32[]{:S(2)}) copy-start(f32[256]{0:T(256)} %param.8) | copy-start | bytes 3076
  40.2 5.2 %copy-start.4 = (f32[256]{0:T(256)S(1)}, f32[256]{0:T(256)}, u32[]{:S(2)}) copy-start(f32[256]{0:T(256)} %param.9) | copy-start | bytes 3076
  57.8 1.6 %collective-permute-start.14 = (f32[9,32,256]{2,1,0:T(8,128)S(1)}, f32[9,32,256]{2,1,0:T(8,128)S(1)}, u32[]{:S(2)}, u32[]{:S(2)}) collective-permute-start(f32[9,32,256]{2,1,0:T(8,128)S(1)} %shard_map.93), channel_id=1, source_target_pairs={{0,1},{1,0},{2,3},{3,2},{4,5},{5,4},{6,7},{7,6},{8,9},{9,8},{10,11... | collective-permute-start | bytes 884744 | tf_op jit(solution)/shard_map/ppermute | solution.py:351
  59.5 9.1 %collective-permute-start.15 = (f32[9,32,256]{2,1,0:T(8,128)S(1)}, f32[9,32,256]{2,1,0:T(8,128)S(1)}, u32[]{:S(2)}, u32[]{:S(2)}) collective-permute-start(f32[9,32,256]{2,1,0:T(8,128)S(1)} %add.35), channel_id=1, source_target_pairs={{0,2},{1,3},{2,0},{3,1},{4,6},{5,7},{6,4},{7,5},{8,10},{9,11},{10,... | collective-permute-start | bytes 884744 | tf_op jit(solution)/shard_map/ppermute | solution.py:351
  68.6 8.3 %collective-permute-start.16 = (f32[9,32,256]{2,1,0:T(8,128)S(1)}, f32[9,32,256]{2,1,0:T(8,128)S(1)}, u32[]{:S(2)}, u32[]{:S(2)}) collective-permute-start(f32[9,32,256]{2,1,0:T(8,128)S(1)} %add.36), channel_id=1, source_target_pairs={{0,4},{4,0},{1,5},{5,1},{2,6},{6,2},{3,7},{7,3},{8,12},{12,8},{9,1... | collective-permute-start | bytes 884744 | tf_op jit(solution)/shard_map/ppermute | solution.py:351
  76.9 24.4 %collective-permute-start.17 = (f32[9,32,256]{2,1,0:T(8,128)S(1)}, f32[9,32,256]{2,1,0:T(8,128)S(1)}, u32[]{:S(2)}, u32[]{:S(2)}) collective-permute-start(f32[9,32,256]{2,1,0:T(8,128)S(1)} %add.37), channel_id=1, source_target_pairs={{0,8},{8,0},{16,24},{24,16},{1,9},{9,1},{17,25},{25,17},{2,10},{10... | collective-permute-start | bytes 884744 | tf_op jit(solution)/shard_map/ppermute | solution.py:351
  79.5 1.2 %collective-permute-start.9 = (f32[40,256]{1,0:T(8,128)S(1)}, f32[40,256]{1,0:T(8,128)S(1)}, u32[]{:S(2)}, u32[]{:S(2)}) collective-permute-start(f32[40,256]{1,0:T(8,128)S(1)} %get-tuple-element.14), channel_id=1, source_target_pairs={{0,1},{1,0},{2,3},{3,2},{4,5},{5,4},{6,7},{7,6},{8,9},{9,8},{10,11... | collective-permute-start | bytes 122888 | tf_op jit(solution)/shard_map/ppermute | solution.py:349
  80.7 4.0 %collective-permute-start.10 = (f32[40,256]{1,0:T(8,128)S(1)}, f32[40,256]{1,0:T(8,128)S(1)}, u32[]{:S(2)}, u32[]{:S(2)}) collective-permute-start(f32[40,256]{1,0:T(8,128)S(1)} %add.30), channel_id=1, source_target_pairs={{0,2},{1,3},{2,0},{3,1},{4,6},{5,7},{6,4},{7,5},{8,10},{9,11},{10,... | collective-permute-start | bytes 122888 | tf_op jit(solution)/shard_map/ppermute | solution.py:349
  84.7 4.0 %collective-permute-start.11 = (f32[40,256]{1,0:T(8,128)S(1)}, f32[40,256]{1,0:T(8,128)S(1)}, u32[]{:S(2)}, u32[]{:S(2)}) collective-permute-start(f32[40,256]{1,0:T(8,128)S(1)} %add.31), channel_id=1, source_target_pairs={{0,4},{4,0},{1,5},{5,1},{2,6},{6,2},{3,7},{7,3},{8,12},{12,8},{9,1... | collective-permute-start | bytes 122888 | tf_op jit(solution)/shard_map/ppermute | solution.py:349
  88.7 4.0 %collective-permute-start.12 = (f32[40,256]{1,0:T(8,128)S(1)}, f32[40,256]{1,0:T(8,128)S(1)}, u32[]{:S(2)}, u32[]{:S(2)}) collective-permute-start(f32[40,256]{1,0:T(8,128)S(1)} %add.32), channel_id=1, source_target_pairs={{0,8},{8,0},{16,24},{24,16},{1,9},{9,1},{17,25},{25,17},{2,10},{10... | collective-permute-start | bytes 122888 | tf_op jit(solution)/shard_map/ppermute | solution.py:349
  92.8 8.6 %collective-permute-start.13 = (f32[40,256]{1,0:T(8,128)S(1)}, f32[40,256]{1,0:T(8,128)S(1)}, u32[]{:S(2)}, u32[]{:S(2)}) collective-permute-start(f32[40,256]{1,0:T(8,128)S(1)} %add.33), channel_id=1, source_target_pairs={{0,16},{8,24},{16,0},{24,8},{1,17},{9,25},{17,1},{25,9},{2,18},{10... | collective-permute-start | bytes 122888 | tf_op jit(solution)/shard_map/ppermute | solution.py:349
  101.4 9.0 %collective-permute-start.18 = (f32[9,32,256]{2,1,0:T(8,128)S(1)}, f32[9,32,256]{2,1,0:T(8,128)S(1)}, u32[]{:S(2)}, u32[]{:S(2)}) collective-permute-start(f32[9,32,256]{2,1,0:T(8,128)S(1)} %add.38), channel_id=1, source_target_pairs={{0,16},{8,24},{16,0},{24,8},{1,17},{9,25},{17,1},{25,9},{2,18},{10... | collective-permute-start | bytes 884744 | tf_op jit(solution)/shard_map/ppermute | solution.py:351
